TPU v7x, 32 devices: a whole 2x2x4 slice. The times are simulated.
32 devices in a mesh: groups: 2 (over y), gx: 16 (over z, x, core).
Axes of the slice: x: 2, y: 2, z: 4, core: 2. Of those that a mesh axis runs over, the one named last changes fastest.
Arguments:
- hidden: bfloat16 [64, 8192], P('groups', 'gx'), parts along dimension 0, may hold values from -6 to 6
- norm_in_gain: float32 [8192], replicated, may hold values from 0.1 to 1.9
- w_z: bfloat16 [8192, 8192], P(None, 'gx'), may hold values from -0.0625 to 0.0625
- w_x: bfloat16 [8192, 8192], P(None, 'gx'), may hold values from -0.0625 to 0.0625
- w_dt: bfloat16 [8192, 128], P(None, 'gx'), may hold values from -0.0625 to 0.0625
- w_bc: bfloat16 [8192, 2048], P(None, 'gx'), may hold values from -0.0625 to 0.0625
- dt_bias: float32 [128], P('gx'), may hold values from -1 to 1
- decay_rate: float32 [128], P('gx'), may hold values from 0.2 to 4
- skip_gain: float32 [128], P('gx'), may hold values from 0.5 to 1.5
- conv_x_weight: float32 [4, 8192], P(None, 'gx'), may hold values from -3 to 3
- conv_bc_weight: float32 [4, 2048], P(None, 'gx'), may hold values from -3 to 3
- conv_x_state: bfloat16 [64, 3, 8192], P('groups', None, 'gx'), parts along dimension 0, may hold values from -6 to 6
- conv_bc_state: bfloat16 [64, 3, 2048], P('groups', None, 'gx'), parts along dimension 0, may hold values from -6 to 6
- ssm_state: float32 [64, 128, 64, 256], P('groups', 'gx'), parts along dimension 0, may hold values from -6 to 6
- group_gain: float32 [8192], P('gx'), may hold values from 0.1 to 1.9
- w_out: bfloat16 [8192, 8192], P('gx'), may hold values from -0.09375 to 0.09375
- norm_mid_gain: float32 [8192], replicated, may hold values from 0.1 to 1.9
- w_up: bfloat16 [8192, 16384], P(None, 'gx'), may hold values from -0.0625 to 0.0625
- w_down: bfloat16 [16384, 8192], P('gx'), may hold values from -0.0625 to 0.0625
Outputs:
- result: bfloat16 [64, 8192], P('groups', 'gx'), parts along dimension 0
- ssm_new: float32 [64, 128, 64, 256], P('groups', 'gx'), parts along dimension 0
- conv_x_new: bfloat16 [64, 3, 8192], P('groups', None, 'gx'), parts along dimension 0
- conv_bc_new: bfloat16 [64, 3, 2048], P('groups', None, 'gx'), parts along dimension 0
There are 2 independent parts, one for each index of `groups`. A program takes and returns all parts, laid end to end along the dimension named above; an argument that names none is the same for every part. Nothing has to cross between parts.
All inputs are finite; a program needn't handle non-finite values.
Results may differ from a plain program's by a relative error of at most 0.0081.
Values may be sent and summed in bfloat16 or wider, within the bound.
A program may use at most 192 MiB of HBM per device.

v0:
```python
import jax
import jax.numpy as jnp
from jax import lax
from jax.sharding import PartitionSpec as P

D = 8192
HEADS = 128
HEAD_DIM = 64
N = 256
G = 4
INNER = 8192


def rms_norm(values, gain_vec):
    inv_scale = lax.rsqrt(jnp.mean(values * values, axis=-1, keepdims=True) + 1e-05)
    return values * inv_scale * gain_vec


def conv_step(conv_state, fresh_cols, weight):
    window = jnp.concatenate([conv_state, fresh_cols[:, None, :]], axis=1)
    conv_sum = jnp.einsum(
        "rkc,kc->rc", window.astype(jnp.float32), weight, precision=lax.Precision.HIGHEST
    )
    return (jax.nn.silu(conv_sum), window[:, 1:])


def body(
    hidden,
    norm_in_gain,
    w_z,
    w_x,
    w_dt,
    w_bc,
    dt_bias,
    decay_rate,
    skip_gain,
    conv_x_weight,
    conv_bc_weight,
    conv_x_state,
    conv_bc_state,
    ssm_state,
    group_gain,
    w_out,
    norm_mid_gain,
    w_up,
    w_down,
):
    position = lax.axis_index("gx")
    width_dev = hidden.shape[1]
    req_rows = hidden.shape[0]
    heads_dev = ssm_state.shape[1]
    full_rows = lax.all_gather(hidden, "gx", axis=1, tiled=True)
    normed = rms_norm(full_rows.astype(jnp.float32), norm_in_gain).astype(jnp.bfloat16)
    gate_z = jnp.dot(normed, w_z, preferred_element_type=jnp.float32)
    step_raw = jnp.dot(normed, w_dt, preferred_element_type=jnp.float32)
    x_raw = jnp.dot(normed, w_x, preferred_element_type=jnp.float32).astype(jnp.bfloat16)
    bc_raw = jnp.dot(normed, w_bc, preferred_element_type=jnp.float32).astype(jnp.bfloat16)
    x_conv, conv_x_new = conv_step(conv_x_state, x_raw, conv_x_weight)
    bc_conv, conv_bc_new = conv_step(conv_bc_state, bc_raw, conv_bc_weight)
    bc_full = lax.all_gather(bc_conv.astype(jnp.bfloat16), "gx", axis=1, tiled=True).astype(
        jnp.float32
    )
    group_idx = position * heads_dev // (HEADS // G)
    b_part = lax.dynamic_slice_in_dim(bc_full, group_idx * N, N, 1)
    c_part = lax.dynamic_slice_in_dim(bc_full, (G + group_idx) * N, N, 1)
    step_size = jax.nn.softplus(step_raw + dt_bias)
    retain = jnp.exp(-step_size * decay_rate)
    x_heads = x_conv.reshape(req_rows, heads_dev, HEAD_DIM)
    ssm_new = (
        retain[:, :, None, None] * ssm_state
        + (step_size[:, :, None] * x_heads)[..., None] * b_part[:, None, None, :]
    )
    head_out = (
        jnp.einsum("rhpn,rn->rhp", ssm_new, c_part, precision=lax.Precision.HIGHEST)
        + skip_gain[None, :, None] * x_heads
    )
    gated_out = head_out.reshape(req_rows, heads_dev * HEAD_DIM) * jax.nn.silu(gate_z)
    onehot = (jnp.arange(G) == group_idx).astype(jnp.float32)
    own_sq = jnp.sum(gated_out * gated_out, axis=-1)
    totals = lax.psum(own_sq[:, None] * onehot[None, :], "gx")
    mean_sq = jnp.sum(totals * onehot[None, :], axis=-1, keepdims=True) / (INNER // G)
    y_normed = (gated_out * lax.rsqrt(mean_sq + 1e-05) * group_gain).astype(jnp.bfloat16)
    mixer_terms = jnp.dot(y_normed, w_out, preferred_element_type=jnp.float32)
    mixer_out = lax.psum_scatter(mixer_terms, "gx", scatter_dimension=1, tiled=True)
    after_mix = (hidden.astype(jnp.float32) + mixer_out).astype(jnp.bfloat16)
    after_f = after_mix.astype(jnp.float32)
    total_sq = lax.psum(jnp.sum(after_f * after_f, axis=-1), "gx")
    gain_own = lax.dynamic_slice_in_dim(norm_mid_gain, position * width_dev, width_dev, 0)
    mid_own = (after_f * lax.rsqrt(total_sq[:, None] / D + 1e-05) * gain_own).astype(jnp.bfloat16)
    hidden_up = jnp.dot(
        lax.all_gather(mid_own, "gx", axis=1, tiled=True), w_up, preferred_element_type=jnp.float32
    )
    active = jnp.square(jnp.maximum(hidden_up, 0.0)).astype(jnp.bfloat16)
    down_sum = lax.psum_scatter(
        jnp.dot(active, w_down, preferred_element_type=jnp.float32),
        "gx",
        scatter_dimension=1,
        tiled=True,
    )
    result = (after_mix.astype(jnp.float32) + down_sum).astype(jnp.bfloat16)
    return (result, ssm_new, conv_x_new, conv_bc_new)


def solution(mesh):
    in_specs = (
        P("groups", "gx"),
        P(),
        P(None, "gx"),
        P(None, "gx"),
        P(None, "gx"),
        P(None, "gx"),
        P("gx"),
        P("gx"),
        P("gx"),
        P(None, "gx"),
        P(None, "gx"),
        P("groups", None, "gx"),
        P("groups", None, "gx"),
        P("groups", "gx", None, None),
        P("gx"),
        P("gx", None),
        P(),
        P(None, "gx"),
        P("gx", None),
    )
    out_specs = (
        P("groups", "gx"),
        P("groups", "gx", None, None),
        P("groups", None, "gx"),
        P("groups", None, "gx"),
    )
    return jax.shard_map(body, mesh=mesh, in_specs=in_specs, out_specs=out_specs, check_vma=False)
```

profile of v0, /device:TPU:0, one launch (start us, length us, event | category | flops | bytes accessed | tf_op | source)
XLA Modules:
  0.0 307.6 jit_solution(10102781608334225628)
XLA Ops:
  7.3 24.9 %all_gather.9 = bf16[32,8192]{1,0:T(8,128)(2,1)S(1)} all-gather(bf16[32,512]{1,0:T(8,128)(2,1)} %param.19), channel_id=1, replica_groups=mesh['groups'=2,'gx'=16] {'gx'}, dimensions={1}, use_global_device_ids=true | all-gather | bytes 557056 | tf_op jit(solution)/shard_map/all_gather | solution.py:52
  32.3 0.2 fusion.4
  32.5 1.2 fusion.3
  33.7 0.8 multiply_reduce_fusion.1
  34.5 17.8 %all_gather.10 = bf16[32,2048]{1,0:T(8,128)(2,1)S(1)} all-gather(bf16[32,128]{1,0:T(8,128)(2,1)S(1)} %fusion.28), channel_id=1, replica_groups=mesh['groups'=2,'gx'=16] {'gx'}, dimensions={1}, use_global_device_ids=true | all-gather | bytes 139264 | tf_op jit(solution)/shard_map/all_gather | solution.py:60
  52.3 5.0 %fusion.2 = bf16[32,1,512]{2,0,1:T(8,128)(2,1)S(1)} fusion(bf16[8192,512]{1,0:T(8,128)(2,1)} %param.22, bf16[32,8192]{1,0:T(8,128)(2,1)S(1)} %all_gather.9, f32[8192]{0:T(1024)} %param.20, f32[32]{0:T(128)S(1)} %add_rsqrt_fusion.2), kind=kOutput, calls=%fused_computation.7 | convolution fusion | flops 269500416 | bytes 8978560 | tf_op jit(solution)/shard_map/dot_general | solution.py:56
  57.5 0.3 multiply_exponential_fusion
  58.0 0.1 broadcast_multiply_fusion
  58.2 7.6 %multiply_add_fusion = f32[32,8,64,256]{3,2,1,0:T(8,128)S(1)} fusion(f32[32,8,64,256]{3,2,1,0:T(8,128)} %param.32, f32[32,256]{1,0:T(8,128)S(1)} %get-tuple-element.7, f32[32,8,64]{2,1,0:T(8,128)S(1)} %broadcast_multiply_fusion, f32[32,8]{1,0:T(8,128)S(1)} %copy.25), kind=kLoop, calls=%fused_computation | loop fusion | flops 12582912 | bytes 33653760 | tf_op jit(solution)/shard_map/add | solution.py:70
  65.8 6.1 %copy-done.2 = f32[32,8,64,256]{3,2,1,0:T(8,128)} copy-done((f32[32,8,64,256]{3,2,1,0:T(8,128)}, f32[32,8,64,256]{3,2,1,0:T(8,128)S(1)}, u32[]{:S(2)}) %copy-start.2) | copy-done | bytes 16777240
  71.9 9.8 %fusion.20 = f32[32,1,8,64]{3,1,2,0:T(1,128)S(1)} fusion(f32[32,8,64,256]{3,2,1,0:T(8,128)S(1)} %multiply_add_fusion, bf16[32,256,1,1]{1,0,2,3:T(8,128)(2,1)S(1)} %get-tuple-element.6), kind=kOutput, calls=%fused_computation.46 | convolution fusion | flops 50331648 | bytes 16859136 | tf_op jit(solution)/shard_map/rhpn,rn->rhp/dot_general | solution.py:74
  81.9 5.1 %multiply_reduce_fusion.2 = (f32[32]{0:T(128)S(1)}, f32[32,512]{1,0:T(8,128)S(1)}) fusion(f32[32,512]{1,0:T(8,128)S(1)} %reshape.55, bf16[8192,512]{1,0:T(8,128)(2,1)} %param.21, bf16[32,8192]{1,0:T(8,128)(2,1)S(1)} %all_gather.9, f32[8192]{0:T(1024)S(1)} %copy-done.3, f32[32]{0:T(128)S(1)} %add_rsqrt_fusion.2), kind=kOutput, calls=%fused_computation.38 | convolution fusion | flops 269598688 | bytes 9076992 | tf_op jit(solution)/shard_map/dot_general | solution.py:54
  87.1 31.1 %psum.14 = f32[32,4]{0,1:T(4,128)S(1)} all-reduce(f32[32,4]{0,1:T(4,128)S(1)} %broadcast_multiply_fusion.1), channel_id=1, replica_groups=mesh['groups'=2,'gx'=16] {'gx'}, use_global_device_ids=true, to_apply=%region_2.3 | all-reduce | flops 128 | bytes 1024 | tf_op jit(solution)/shard_map/psum | solution.py:80
  118.3 6.0 %fusion.19 = f32[32,8192]{1,0:T(8,128)} fusion(bf16[512,8192]{1,0:T(8,128)(2,1)} %param.34, f32[512]{0:T(512)S(1)} %copy-done.7, f32[32]{0:T(128)S(1)} %add_rsqrt_fusion.1, f32[32,512]{1,0:T(8,128)S(1)} %reshape.55, f32[32,512]{1,0:T(8,128)S(1)} %get-tuple-element.11), kind=kOutput, calls=%fused_computation.45 | convolution fusion | flops 268566528 | bytes 9570432 | tf_op jit(solution)/shard_map/dot_general | solution.py:83
  124.4 0.8 dynamic_slice.11
  125.1 53.9 %reduce-scatter.3.cloned.1.call-done = f32[32,512]{1,0:T(8,128)} async-done(((f32[32,8192]{1,0:T(8,128)}), f32[32,512]{1,0:T(8,128)}) %reduce-scatter.3.cloned.1.call-update) | async-done | bytes 65552 | tf_op jit(solution)/shard_map/reduce_scatter | solution.py:84
  179.1 1.0 fusion.10
  180.1 29.6 %psum.15 = f32[32]{0:T(128)S(1)} all-reduce(f32[32]{0:T(128)S(1)} %get-tuple-element.4), channel_id=1, replica_groups=mesh['groups'=2,'gx'=16] {'gx'}, use_global_device_ids=true, to_apply=%region_6.7 | all-reduce | flops 32 | bytes 256 | tf_op jit(solution)/shard_map/psum | solution.py:87
  209.7 18.9 %all_gather.11 = bf16[32,8192]{1,0:T(8,128)(2,1)S(1)} all-gather(bf16[32,512]{1,0:T(8,128)(2,1)S(1)} %fusion.12), channel_id=1, replica_groups=mesh['groups'=2,'gx'=16] {'gx'}, dimensions={1}, use_global_device_ids=true | all-gather | bytes 557056 | tf_op jit(solution)/shard_map/all_gather | solution.py:91
  228.6 14.6 %fusion.7 = f32[32,8192]{1,0:T(8,128)} fusion(bf16[1024,8192]{1,0:T(8,128)(2,1)} %param.37, bf16[32,8192]{1,0:T(8,128)(2,1)S(1)} %all_gather.11, bf16[8192,1024]{1,0:T(8,128)(2,1)} %param.36), kind=kOutput, calls=%fused_computation.14 | convolution fusion | flops 1073840128 | bytes 35127296 | tf_op jit(solution)/shard_map/dot_general | solution.py:95
  243.2 0.6 fusion.24
  243.9 0.7 fusion.9
  244.5 54.8 %reduce-scatter.5.cloned.1.call-done = f32[32,512]{1,0:T(8,128)} async-done(((f32[32,8192]{1,0:T(8,128)}), f32[32,512]{1,0:T(8,128)}) %reduce-scatter.5.cloned.1.call-update) | async-done | bytes 65552 | tf_op jit(solution)/shard_map/reduce_scatter | solution.py:94
  299.3 1.5 fusion.13
  (45 shorter events, 0.9 us)
Async XLA Ops:
  7.2 25.3 %copy-start = (bf16[8192,128]{1,0:T(8,128)(2,1)S(1)}, bf16[8192,128]{1,0:T(8,128)(2,1)}, u32[]{:S(2)}) copy-start(bf16[8192,128]{1,0:T(8,128)(2,1)} %param.24) | copy-start | bytes 6291460
  7.2 50.3 %copy-start.3 = (f32[8192]{0:T(1024)S(1)}, f32[8192]{0:T(1024)}, u32[]{:S(2)}) copy-start(f32[8192]{0:T(1024)} %param.20) | copy-start | bytes 98308
  7.2 50.1 %copy-start.8 = (f32[4,512]{1,0:T(4,128)S(1)}, f32[4,512]{1,0:T(4,128)}, u32[]{:S(2)}) copy-start(f32[4,512]{1,0:T(4,128)} %param.28) | copy-start | bytes 24580
  7.2 50.1 %copy-start.4 = (bf16[32,3,512]{2,0,1:T(8,128)(2,1)S(1)}, bf16[32,3,512]{2,0,1:T(8,128)(2,1)}, u32[]{:S(2)}) copy-start(bf16[32,3,512]{2,0,1:T(8,128)(2,1)} %param.30) | copy-start | bytes 294916
  7.2 50.3 %copy-start.10 = (bf16[8192,8]{0,1:T(8,128)(2,1)S(1)}, bf16[8192,8]{0,1:T(8,128)(2,1)}, u32[]{:S(2)}) copy-start(bf16[8192,8]{0,1:T(8,128)(2,1)} %param.23) | copy-start | bytes 393220
  7.2 50.3 %copy-start.12 = (f32[8]{0:T(128)S(1)}, f32[8]{0:T(128)}, u32[]{:S(2)}) copy-start(f32[8]{0:T(128)} %param.25) | copy-start | bytes 100
  7.2 50.3 %copy-start.11 = (f32[8]{0:T(128)S(1)}, f32[8]{0:T(128)}, u32[]{:S(2)}) copy-start(f32[8]{0:T(128)} %param.26) | copy-start | bytes 100
  7.2 171.8 %reduce-scatter.3.cloned.1.call-start = ((), (), s32[]{:S(2)}) async-start(), calls=%async_computation.2 | async-start | bytes 1114112 | tf_op jit(solution)/shard_map/reduce_scatter | solution.py:84
  65.7 6.2 %copy-start.2 = (f32[32,8,64,256]{3,2,1,0:T(8,128)}, f32[32,8,64,256]{3,2,1,0:T(8,128)S(1)}, u32[]{:S(2)}) copy-start(f32[32,8,64,256]{3,2,1,0:T(8,128)S(1)} %multiply_add_fusion) | copy-start | bytes 50331652
  65.7 16.0 %copy-start.9 = (f32[8]{0:T(128)S(1)}, f32[8]{0:T(128)}, u32[]{:S(2)}) copy-start(f32[8]{0:T(128)} %param.27) | copy-start | bytes 100
  71.9 46.4 %copy-start.7 = (f32[512]{0:T(512)S(1)}, f32[512]{0:T(512)}, u32[]{:S(2)}) copy-start(f32[512]{0:T(512)} %param.33) | copy-start | bytes 6148
  81.7 97.3 %copy-start.5 = (bf16[32,512]{1,0:T(8,128)(2,1)S(1)}, bf16[32,512]{1,0:T(8,128)(2,1)}, u32[]{:S(2)}) copy-start(bf16[32,512]{1,0:T(8,128)(2,1)} %param.19) | copy-start | bytes 98308
  124.3 175.0 %reduce-scatter.5.cloned.1.call-start = ((), (), s32[]{:S(2)}) async-start(), calls=%async_computation.3 | async-start | bytes 1114112 | tf_op jit(solution)/shard_map/reduce_scatter | solution.py:94
  209.7 91.1 %copy-start.1 = (bf16[8192,128]{1,0:T(8,128)(2,1)S(1)}, bf16[8192,128]{1,0:T(8,128)(2,1)}, u32[]{:S(2)}) copy-start(bf16[8192,128]{1,0:T(8,128)(2,1)} %param.24) | copy-start | bytes 6291460
  228.6 14.6 %copy-start.6 = (bf16[32,3,128]{2,0,1:T(8,128)(2,1)S(1)}, bf16[32,3,128]{2,0,1:T(8,128)(2,1)}, u32[]{:S(2)}) copy-start(bf16[32,3,128]{2,0,1:T(8,128)(2,1)} %param.31) | copy-start | bytes 73732
Sparse Core Ops, SparseCore 0:
  124.4 54.5 reduce-scatter.2
  243.4 55.9 reduce-scatter.4
where the time goes:
time: 308 us
  blocking collectives  122 us (40%)
  waiting for transfers between devices  109 us (35%)
  matrix products  42.1 us (14%)
  between operations  14.3 us (5%)
  other arithmetic  12.8 us (4%)
  local copies, waits for them, and re-layouts  7.3 us (2%)
    reduce_scatter x1, waiting for transfers between devices, body(): lax.psum_scatter(jnp.dot(active, w_down, preferred_element_type=jnp.float...  54.8 us
    reduce_scatter x1, waiting for transfers between devices, body(): lax.psum_scatter(mixer_terms, 'gx', scatter_dimension=1, tiled=True)  53.9 us
    psum x1, blocking collectives, body(): totals = lax.psum(own_sq[:, None] * onehot[None, :], 'gx')  31.1 us
    psum x1, blocking collectives, body(): total_sq = lax.psum(jnp.sum(after_f * after_f, axis=-1), 'gx')  29.6 us
    all_gather x1, blocking collectives, body(): full_rows = lax.all_gather(hidden, 'gx', axis=1, tiled=True)  24.9 us
    all_gather x1, blocking collectives, body(): lax.all_gather(mid_own, 'gx', axis=1, tiled=True)  18.9 us
    all_gather x1, blocking collectives, body(): lax.all_gather(bc_conv.astype(jnp.bfloat16), 'gx', axis=1, tiled=True)  17.8 us
    dot_general x1, matrix products, body(): jnp.dot(active, w_down, preferred_element_type=jnp.float32)  14.6 us
  transfers between devices with their start and end apart: 2, of which 2 were waited for; matrix products, arithmetic and copies ran while one was open for 1% of the time, Pallas kernels for 0%

commit v1 on v0

--- a/solution.py
+++ b/solution.py
@@ -1,6 +1,10 @@
+import functools
+
 import jax
 import jax.numpy as jnp
 from jax import lax
+from jax.experimental import pallas as pl
+from jax.experimental.pallas import tpu as pltpu
 from jax.sharding import PartitionSpec as P
 
 D = 8192
@@ -24,7 +28,7 @@
     return (jax.nn.silu(conv_sum), window[:, 1:])
 
 
-def body(
+def plain_body(
     hidden,
     norm_in_gain,
     w_z,
@@ -101,6 +105,385 @@
     return (result, ssm_new, conv_x_new, conv_bc_new)
 
 
+MESH = pl.DeviceIdType.MESH
+NDEV = 16
+LINES = 4
+F32 = jnp.float32
+BF16 = jnp.bfloat16
+VM = pl.BlockSpec(memory_space=pltpu.VMEM)
+HB = pl.BlockSpec(memory_space=pl.ANY)
+
+
+def spot(z, x, c):
+    return z * 4 + x * 2 + c
+
+
+def coords():
+    me = lax.axis_index("gx")
+    return me, me // 4, (me // 2) % 2, me % 2
+
+
+def remote(src, dst, send, recv, dev):
+    return pltpu.make_async_remote_copy(
+        src_ref=src, dst_ref=dst, send_sem=send, recv_sem=recv,
+        device_id={"gx": dev}, device_id_type=MESH,
+    )
+
+
+def greet(me):
+    barrier = pltpu.get_barrier_semaphore()
+    for i in range(1, NDEV):
+        pl.semaphore_signal(
+            barrier, inc=1, device_id={"gx": (me + i) % NDEV}, device_id_type=MESH
+        )
+    pl.semaphore_wait(barrier, NDEV - 1)
+
+
+def gather_blocks(blocks, send, recv):
+    me, z, x, c = coords()
+    started = []
+
+    def put(b, dev):
+        cp = remote(blocks.at[b], blocks.at[b], send.at[len(started)], recv.at[b], dev)
+        cp.start()
+        started.append(cp)
+
+    def arrive(b):
+        remote(blocks.at[b], blocks.at[b], send.at[0], recv.at[b], (me + 1) % NDEV).wait_recv()
+
+    across, beside = spot(z, 1 - x, c), spot(z, x, 1 - c)
+    for dz in (2, 1, 3):
+        put(me, spot((z + dz) % LINES, x, c))
+    put(me, across)
+    put(me, beside)
+    for dz in (1, 3, 2):
+        b = spot((z + dz) % LINES, x, c)
+        arrive(b)
+        put(b, across)
+        put(b, beside)
+    for dz in (0, 1, 3, 2):
+        b = spot((z + dz) % LINES, 1 - x, c)
+        arrive(b)
+        put(b, beside)
+    for dz in (0, 1, 3, 2):
+        arrive(spot((z + dz) % LINES, x, 1 - c))
+        arrive(spot((z + dz) % LINES, 1 - x, 1 - c))
+    return started
+
+
+def norm_blocks(blocks, gain_ref, out):
+    width = blocks.shape[2]
+    total = jnp.zeros(blocks.shape[1:], F32)
+    for k in range(NDEV):
+        v = blocks[k].astype(F32)
+        total += v * v
+    inv = lax.rsqrt(jnp.sum(total, axis=1, keepdims=True) / (NDEV * width) + 1e-05)
+    for k in range(NDEV):
+        out[k] = (blocks[k].astype(F32) * inv * gain_ref[:, k * width : (k + 1) * width]).astype(BF16)
+
+
+def spread_sum(part_fn, scale_fn, parts, csend, crecv, xsend, xrecv, zsend, zrecv, sems):
+    me, z, x, c = coords()
+    across, beside = spot(z, 1 - x, c), spot(z, x, 1 - c)
+    cs, cr, xs, xr, zs, zr = sems
+    ccp, xcp, zcp = {}, {}, {}
+    own = None
+    for step in range(LINES + 2):
+        t = step
+        if t < LINES:
+            part_fn(t, parts)
+            for xx in range(2):
+                csend[t, xx] = parts[t, xx * 2 + (1 - c)].astype(BF16)
+            ccp[t] = remote(csend.at[t], crecv.at[t], cs.at[t], cr.at[t], beside)
+            ccp[t].start()
+        t = step - 1
+        if 0 <= t < LINES:
+            ccp[t].wait_recv()
+            xsend[t] = (parts[t, (1 - x) * 2 + c] + crecv[t, 1 - x].astype(F32)).astype(BF16)
+            xcp[t] = remote(xsend.at[t], xrecv.at[t], xs.at[t], xr.at[t], across)
+            xcp[t].start()
+        t = step - 2
+        if 0 <= t < LINES:
+            xcp[t].wait_recv()
+            v = parts[t, x * 2 + c] + crecv[t, x].astype(F32) + xrecv[t].astype(F32)
+            v = scale_fn(v)
+            if t < LINES - 1:
+                zsend[t] = v.astype(BF16)
+                zcp[t] = remote(
+                    zsend.at[t], zrecv.at[t], zs.at[t], zr.at[t], spot((z + 1 + t) % LINES, x, c)
+                )
+                zcp[t].start()
+            else:
+                own = v
+    for t in range(LINES - 1):
+        zcp[t].wait_recv()
+        own = own + zrecv[t].astype(F32)
+    return own, list(ccp.values()) + list(xcp.values()) + list(zcp.values())
+
+
+def conv_rows(state_ref, fresh, weight_ref, new_ref):
+    total = fresh.astype(F32) * weight_ref[3:4, :]
+    for k in range(3):
+        total += state_ref[k].astype(F32) * weight_ref[k : k + 1, :]
+    new_ref[0] = state_ref[1]
+    new_ref[1] = state_ref[2]
+    new_ref[2] = fresh
+    return total / (1.0 + jnp.exp(-total))
+
+
+def front_kernel(
+    hid, gain, wz, wx, wbc, wdt, dtb, dec, cxw, cbw, cxs, cbs,
+    xconv, gate, step, retain, bc, cxn, cbn,
+    blocks, xn, wz_v, wx_v, wbc_v, bc_own, bc_got,
+    wsem, bsem, ag_s, ag_r, bc_s, bc_r,
+):
+    me, z, x, c = coords()
+    rows = wx_v.shape[1]
+    bc_cp = pltpu.make_async_copy(wbc, wbc_v, bsem)
+    bc_cp.start()
+    loads = []
+    for i, (src, dst) in enumerate(((wx, wx_v), (wz, wz_v))):
+        for k in range(4):
+            cp = pltpu.make_async_copy(
+                src.at[pl.ds(k * rows, rows), :], dst.at[k], wsem.at[i * 4 + k]
+            )
+            cp.start()
+            loads.append(cp)
+    blocks[me] = hid[...]
+    greet(me)
+    started = gather_blocks(blocks, ag_s, ag_r)
+    norm_blocks(blocks, gain, xn)
+    width = hid.shape[1]
+
+    bc_cp.wait()
+    acc = jnp.zeros(bc_own.shape, F32)
+    for k in range(NDEV):
+        acc += jnp.dot(xn[k], wbc_v[k * width : (k + 1) * width, :], preferred_element_type=F32)
+    bc_own[...] = conv_rows(cbs, acc.astype(BF16), cbw, cbn).astype(BF16)
+    goal, slot = (me % 8) // 2, (me // 8) * 2 + me % 2
+    for i in range(4):
+        dev = goal * 4 + i
+
+        @pl.when(dev != me)
+        def _():
+            remote(bc_own, bc_got.at[slot], bc_s.at[i], bc_r.at[slot], dev).start()
+
+        @pl.when(dev == me)
+        def _():
+            bc_got[slot] = bc_own[...]
+
+    def project(w_v, first):
+        acc = jnp.zeros(xconv.shape, F32)
+        for k in range(4):
+            loads[first + k].wait()
+            for j in range(4):
+                acc += jnp.dot(
+                    xn[k * 4 + j], w_v[k, j * width : (j + 1) * width, :],
+                    preferred_element_type=F32,
+                )
+        return acc
+
+    acc = jnp.zeros(step.shape, F32)
+    for k in range(NDEV):
+        acc += lax.dot_general(
+            xn[k], wdt[:, k * width : (k + 1) * width], (((1,), (1,)), ((), ())),
+            preferred_element_type=F32,
+        )
+    raw = acc + dtb[...]
+    size = jnp.maximum(raw, 0.0) + jnp.log1p(jnp.exp(-jnp.abs(raw)))
+    step[...] = size
+    retain[...] = jnp.exp(-size * dec[...])
+    xconv[...] = conv_rows(cxs, project(wx_v, 0).astype(BF16), cxw, cxn)
+    zv = project(wz_v, 4)
+    gate[...] = zv / (1.0 + jnp.exp(-zv))
+
+    for i in range(4):
+        src = (i // 2) * 8 + z * 2 + i % 2
+
+        @pl.when(src != me)
+        def _():
+            remote(bc_own, bc_got.at[i], bc_s.at[0], bc_r.at[i], src).wait_recv()
+
+    bc[...] = bc_got[...]
+    for i in range(4):
+        dev = goal * 4 + i
+
+        @pl.when(dev != me)
+        def _():
+            remote(bc_own, bc_got.at[slot], bc_s.at[i], bc_r.at[slot], dev).wait_send()
+
+    for cp in started:
+        cp.wait_send()
+
+
+def back_kernel(
+    gated, ggain, hid, mgain, wo, wu, wd,
+    result,
+    wo_v, wu_v, wd_v, y, act, parts, blocks, xn, sq_own, sq_got,
+    csend, crecv, xsend, xrecv, zsend, zrecv,
+    wsem, sq_s, sq_r, ag_s, ag_r, rs1, rs2,
+):
+    me, z, x, c = coords()
+    cols = wo_v.shape[2]
+    rows = wu_v.shape[1]
+    width = hid.shape[1]
+    loads = {}
+    for t in range(LINES):
+        at = pl.multiple_of(((z + 1 + t) % LINES) * cols, cols)
+        loads["o", t] = pltpu.make_async_copy(wo.at[:, pl.ds(at, cols)], wo_v.at[t], wsem.at[t])
+    for t in range(LINES):
+        loads["u", t] = pltpu.make_async_copy(
+            wu.at[pl.ds(t * rows, rows), :], wu_v.at[t], wsem.at[4 + t]
+        )
+    for t in range(LINES):
+        at = pl.multiple_of(((z + 1 + t) % LINES) * cols, cols)
+        loads["d", t] = pltpu.make_async_copy(wd.at[:, pl.ds(at, cols)], wd_v.at[t], wsem.at[8 + t])
+    for cp in loads.values():
+        cp.start()
+    g = gated[...]
+    y[...] = (g * ggain[...]).astype(BF16)
+    sq_own[...] = jnp.broadcast_to(jnp.sum(g * g, axis=1, keepdims=True), sq_own.shape)
+    greet(me)
+    mates = (spot(z, x, 1 - c), spot(z, 1 - x, c), spot(z, 1 - x, 1 - c))
+    sq_cp = [remote(sq_own, sq_got.at[i], sq_s.at[i], sq_r.at[i], mates[i]) for i in range(3)]
+    for cp in sq_cp:
+        cp.start()
+    scale = []
+
+    def group_scale(v):
+        if not scale:
+            total = sq_own[...]
+            for i in range(3):
+                sq_cp[i].wait_recv()
+                total = total + sq_got[i]
+            scale.append(lax.rsqrt(total[:, :1] / (4 * width) + 1e-05))
+        return v * scale[0]
+
+    def part(name, lhs, w_v):
+        def fn(t, out):
+            loads[name, t].wait()
+            for b in range(4):
+                out[t, b] = jnp.dot(
+                    lhs[...], w_v[t, :, b * width : (b + 1) * width], preferred_element_type=F32
+                )
+        return fn
+
+    mix, started = spread_sum(
+        part("o", y, wo_v), group_scale, parts,
+        csend.at[0], crecv.at[0], xsend.at[0], xrecv.at[0], zsend.at[0], zrecv.at[0],
+        [rs1.at[i] for i in range(6)],
+    )
+    after = (hid[...].astype(F32) + mix).astype(BF16)
+    blocks[me] = after
+    started += sq_cp + gather_blocks(blocks, ag_s, ag_r)
+    norm_blocks(blocks, mgain, xn)
+    acc = jnp.zeros(act.shape, F32)
+    for t in range(LINES):
+        loads["u", t].wait()
+        for j in range(4):
+            acc += jnp.dot(
+                xn[t * 4 + j], wu_v[t, j * width : (j + 1) * width, :], preferred_element_type=F32
+            )
+    act[...] = jnp.square(jnp.maximum(acc, 0.0)).astype(BF16)
+    down, more = spread_sum(
+        part("d", act, wd_v), lambda v: v, parts,
+        csend.at[1], crecv.at[1], xsend.at[1], xrecv.at[1], zsend.at[1], zrecv.at[1],
+        [rs2.at[i] for i in range(6)],
+    )
+    result[...] = (blocks[me].astype(F32) + down).astype(BF16)
+    for cp in started + more:
+        cp.wait_send()
+
+
+def body(
+    hidden, norm_in_gain, w_z, w_x, w_dt, w_bc, dt_bias, decay_rate, skip_gain,
+    conv_x_weight, conv_bc_weight, conv_x_state, conv_bc_state, ssm_state,
+    group_gain, w_out, norm_mid_gain, w_up, w_down,
+):
+    req, width = hidden.shape
+    dim = w_x.shape[0]
+    heads_dev = ssm_state.shape[1]
+    inner = w_x.shape[1]
+    bcw = w_bc.shape[1]
+    ff = w_up.shape[1]
+    dma = pltpu.SemaphoreType.DMA
+    xconv, gate, step, retain, bc, cxn, cbn = pl.pallas_call(
+        front_kernel,
+        out_shape=[
+            jax.ShapeDtypeStruct((req, inner), F32),
+            jax.ShapeDtypeStruct((req, inner), F32),
+            jax.ShapeDtypeStruct((req, heads_dev), F32),
+            jax.ShapeDtypeStruct((req, heads_dev), F32),
+            jax.ShapeDtypeStruct((4, req, bcw), BF16),
+            jax.ShapeDtypeStruct((3, req, inner), BF16),
+            jax.ShapeDtypeStruct((3, req, bcw), BF16),
+        ],
+        in_specs=[VM, VM, HB, HB, HB] + [VM] * 7,
+        out_specs=[VM] * 7,
+        scratch_shapes=[
+            pltpu.VMEM((NDEV, req, width), BF16),
+            pltpu.VMEM((NDEV, req, width), BF16),
+            pltpu.VMEM((4, dim // 4, inner), BF16),
+            pltpu.VMEM((4, dim // 4, inner), BF16),
+            pltpu.VMEM((dim, bcw), BF16),
+            pltpu.VMEM((req, bcw), BF16),
+            pltpu.VMEM((4, req, bcw), BF16),
+            dma((8,)), dma, dma((15,)), dma((16,)), dma((4,)), dma((4,)),
+        ],
+        compiler_params=pltpu.CompilerParams(
+            collective_id=0, has_side_effects=True, vmem_limit_bytes=32 << 20
+        ),
+        name="front",
+    )(
+        hidden, norm_in_gain[None], w_z, w_x, w_bc, w_dt.T, dt_bias[None], decay_rate[None],
+        conv_x_weight, conv_bc_weight,
+        conv_x_state.transpose(1, 0, 2), conv_bc_state.transpose(1, 0, 2),
+    )
+    b_part = jnp.concatenate([bc[0], bc[1]], axis=1).astype(F32)
+    c_part = jnp.concatenate([bc[2], bc[3]], axis=1).astype(F32)
+    x_heads = xconv.reshape(req, heads_dev, HEAD_DIM)
+    ssm_new = (
+        retain[:, :, None, None] * ssm_state
+        + (step[:, :, None] * x_heads)[..., None] * b_part[:, None, None, :]
+    )
+    head_out = (
+        jnp.einsum("rhpn,rn->rhp", ssm_new, c_part, precision=lax.Precision.HIGHEST)
+        + skip_gain[None, :, None] * x_heads
+    )
+    gated = head_out.reshape(req, inner) * gate
+    slot = (LINES, req, width)
+    result = pl.pallas_call(
+        back_kernel,
+        out_shape=jax.ShapeDtypeStruct((req, width), BF16),
+        in_specs=[VM] * 4 + [HB] * 3,
+        out_specs=VM,
+        scratch_shapes=[
+            pltpu.VMEM((4, inner, dim // 4), BF16),
+            pltpu.VMEM((4, dim // 4, ff), BF16),
+            pltpu.VMEM((4, ff, dim // 4), BF16),
+            pltpu.VMEM((req, inner), BF16),
+            pltpu.VMEM((req, ff), BF16),
+            pltpu.VMEM((4, 4, req, width), F32),
+            pltpu.VMEM((NDEV, req, width), BF16),
+            pltpu.VMEM((NDEV, req, width), BF16),
+            pltpu.VMEM((req, 128), F32),
+            pltpu.VMEM((3, req, 128), F32),
+            pltpu.VMEM((2, 4, 2, req, width), BF16),
+            pltpu.VMEM((2, 4, 2, req, width), BF16),
+            pltpu.VMEM((2,) + slot, BF16),
+            pltpu.VMEM((2,) + slot, BF16),
+            pltpu.VMEM((2,) + slot, BF16),
+            pltpu.VMEM((2,) + slot, BF16),
+            dma((12,)), dma((3,)), dma((3,)), dma((15,)), dma((16,)), dma((6, 4)), dma((6, 4)),
+        ],
+        compiler_params=pltpu.CompilerParams(
+            collective_id=1, has_side_effects=True, vmem_limit_bytes=52 << 20
+        ),
+        name="back",
+    )(gated, group_gain[None], hidden, norm_mid_gain[None], w_out, w_up, w_down)
+    return (result, ssm_new, cxn.transpose(1, 0, 2), cbn.transpose(1, 0, 2))
+
+
 def solution(mesh):
     in_specs = (
         P("groups", "gx"),
@@ -129,4 +512,5 @@
         P("groups", None, "gx"),
         P("groups", None, "gx"),
     )
-    return jax.shard_map(body, mesh=mesh, in_specs=in_specs, out_specs=out_specs, check_vma=False)
+    chosen = body if mesh.shape["gx"] == NDEV else plain_body
+    return jax.shard_map(chosen, mesh=mesh, in_specs=in_specs, out_specs=out_specs, check_vma=False)

time: 308 us -> 101 us (0.33)
  blocking collectives: 122 us -> 0 us
  waiting for transfers between devices: 109 us -> 0 us
  Pallas kernels: 0 us -> 58.5 us
  matrix products: 42.1 us -> 9.84 us
  local copies, waits for them, and re-layouts: 7.3 us -> 23.3 us
  between operations: 14.3 us -> 0.77 us
  other arithmetic: 12.8 us -> 7.86 us
    reduce_scatter x2 -> x0, waiting for transfers between devices: 109 us -> none  [the longest x1 54.8 us: body(): lax.psum_scatter(jnp.dot(active, w_down, preferred_element_type=jnp.float...]
    all_gather x3 -> x0, blocking collectives: 61.6 us -> none  [the longest x1 24.9 us: body(): full_rows = lax.all_gather(hidden, 'gx', axis=1, tiled=True)]
    psum x2 -> x0, blocking collectives: 60.7 us -> none  [the longest x1 31.1 us: body(): totals = lax.psum(own_sq[:, None] * onehot[None, :], 'gx')]
    pallas_call x0 -> x2, Pallas kernels: none -> 58.5 us  [the longest x1 39.7 us: body(): pl.pallas_call(back_kernel, out_shape=jax.ShapeDtypeStruct((req, width),...]
    dot_general x6 -> x0, matrix products: 32.3 us -> none  [the longest x1 14.6 us: body(): jnp.dot(active, w_down, preferred_element_type=jnp.float32)]
    unnamed x26 -> x37, local copies, waits for them, and re-layouts: 6.21 us -> 23.1 us
  transfers between devices with their start and end apart: 2 -> 0, of which waited for: 2 -> 0; matrix products, arithmetic and copies ran while one was open for 1% -> 0% of each run, Pallas kernels for 0% -> 0%
where the time goes in v1:
time: 101 us; the launch traced here: 100 us
  Pallas kernels  58.5 us (58%)
  local copies, waits for them, and re-layouts  23.3 us (23%)
  matrix products  9.84 us (10%)
  other arithmetic  7.86 us (8%)
    pallas_call x1, Pallas kernels, body(): pl.pallas_call(back_kernel, out_shape=jax.ShapeDtypeStruct((req, width),...  39.7 us
    unnamed x37, local copies, waits for them, and re-layouts  23.1 us
    pallas_call x1, Pallas kernels, body(): pl.pallas_call(front_kernel, out_shape=[jax.ShapeDtypeStruct((req, inner)...  18.9 us
    dot_general x1, matrix products, body(): jnp.einsum('rhpn,rn->rhp', ssm_new, c_part, precision=lax.Precision.HIGHEST)  9.84 us
    add x1, other arithmetic, body(): retain[:, :, None, None] * ssm_state  7.65 us

profile of v1, /device:TPU:0, one launch (start us, length us, event | category | flops | bytes accessed | tf_op | source)
XLA Modules:
  0.0 100.3 jit_solution(15477562134308343774)
XLA Ops:
  0.6 3.4 %copy-done = bf16[8192,512]{1,0:T(8,128)(2,1)S(1)} copy-done((bf16[8192,512]{1,0:T(8,128)(2,1)S(1)}, bf16[8192,512]{1,0:T(8,128)(2,1)}, u32[]{:S(2)}) %copy-start) | copy-done | bytes 8388632
  4.0 3.4 %copy-done.1 = bf16[8192,512]{1,0:T(8,128)(2,1)S(1)} copy-done((bf16[8192,512]{1,0:T(8,128)(2,1)S(1)}, bf16[8192,512]{1,0:T(8,128)(2,1)}, u32[]{:S(2)}) %copy-start.1) | copy-done | bytes 8388632
  7.4 1.6 %copy-done.2 = bf16[8192,128]{1,0:T(8,128)(2,1)S(1)} copy-done((bf16[8192,128]{1,0:T(8,128)(2,1)S(1)}, bf16[8192,128]{1,0:T(8,128)(2,1)}, u32[]{:S(2)}) %copy-start.2) | copy-done | bytes 2097176
  9.0 0.9 copy-done.3
  9.9 0.8 copy-done.4
  10.7 0.9 copy-done.6
  11.6 0.8 copy-done.7
  12.3 0.7 copy-done.9
  13.0 0.7 copy-done.10
  13.7 0.7 copy-done.11
  14.4 0.7 copy-done.13
  15.1 0.7 copy-done.14
  15.7 18.9 %front.1 = (f32[32,512]{1,0:T(8,128)S(1)}, f32[32,512]{1,0:T(8,128)S(1)}, f32[32,8]{1,0:T(8,128)S(1)}, f32[32,8]{1,0:T(8,128)S(1)}, bf16[4,32,128]{2,1,0:T(8,128...) custom-call(bf16[32,512]{1,0:T(8,128)(2,1)S(1)} %copy-done.4, f32[1,8192]{1,0:T(1,128)S(1)} %bitcast.26, ...), custom_call_target="tpu_custom_call" | custom-call | tf_op jit(solution)/shard_map/front/pallas_call | solution.py:410
  34.7 0.1 reshape.39
  34.8 0.1 broadcast_multiply_fusion
  34.9 7.7 %multiply_add_fusion = f32[32,8,64,256]{3,2,1,0:T(8,128)S(1)} fusion(f32[32,8,64,256]{3,2,1,0:T(8,128)} %param.32, f32[32,256]{1,0:T(8,128)S(1)} %maximum_convert_fusion, f32[32,8,64]{2,1,0:T(8,128)S(1)} %broadcast_multiply_fusion, f32[32,8]{1,0:T(8,128)S(1)} %get-tuple-element.11), kind=kLoop, calls=%fused_computation | loop fusion | flops 12582912 | bytes 33653760 | tf_op jit(solution)/shard_map/add | solution.py:446
  42.5 6.2 %copy-done.15 = f32[32,8,64,256]{3,2,1,0:T(8,128)} copy-done((f32[32,8,64,256]{3,2,1,0:T(8,128)}, f32[32,8,64,256]{3,2,1,0:T(8,128)S(1)}, u32[]{:S(2)}) %copy-start.15) | copy-done | bytes 16777240
  48.7 9.8 %fusion = f32[32,1,8,64]{3,1,2,0:T(1,128)S(1)} fusion(f32[32,8,64,256]{3,2,1,0:T(8,128)S(1)} %multiply_add_fusion, bf16[32,256,1,1]{1,0,2,3:T(8,128)(2,1)S(1)} %maximum_bitcast_fusion), kind=kOutput, calls=%fused_computation.3 | convolution fusion | flops 50331648 | bytes 16859136 | tf_op jit(solution)/shard_map/rhpn,rn->rhp/dot_general | solution.py:450
  58.5 0.1 multiply_add_fusion.1
  58.6 0.1 reshape.40
  58.8 39.7 %back.1 = bf16[32,512]{1,0:T(8,128)(2,1)S(1)} custom-call(f32[32,512]{1,0:T(8,128)S(1)} %mul.53.gated, f32[1,512]{1,0:T(1,128)S(1)} %bitcast.30, bf16[32,512]{1,0:T(8,128)(2,1)S(1)} %copy-done.5, f32[1,8192]{1,0:T(1,128)S(1)} %bitcast.27, bf16[512,8192]{1,0:T(8,128)(2,1)} %wo.1, bf16[8192,1024]{1,0:T(8,128)(2,1)} %wu.1, bf16[1024,8192]{1,0:T(8,128)(2,1)} %wd.1), custom_call_target="tpu_custom_call" | custom-call | tf_op jit(solution)/shard_map/back/pallas_call | solution.py:455
  98.4 0.6 copy.30
  99.1 0.6 copy.31
  99.7 0.6 copy.32
  (25 shorter events, 0.1 us)
Async XLA Ops:
  0.6 3.4 %copy-start = (bf16[8192,512]{1,0:T(8,128)(2,1)S(1)}, bf16[8192,512]{1,0:T(8,128)(2,1)}, u32[]{:S(2)}) copy-start(bf16[8192,512]{1,0:T(8,128)(2,1)} %wz.1) | copy-start | bytes 25165828
  4.0 3.4 %copy-start.1 = (bf16[8192,512]{1,0:T(8,128)(2,1)S(1)}, bf16[8192,512]{1,0:T(8,128)(2,1)}, u32[]{:S(2)}) copy-start(bf16[8192,512]{1,0:T(8,128)(2,1)} %wx.1) | copy-start | bytes 25165828
  7.4 1.6 %copy-start.2 = (bf16[8192,128]{1,0:T(8,128)(2,1)S(1)}, bf16[8192,128]{1,0:T(8,128)(2,1)}, u32[]{:S(2)}) copy-start(bf16[8192,128]{1,0:T(8,128)(2,1)} %wbc.1) | copy-start | bytes 6291460
  9.0 0.9 copy-start.3
  9.9 0.8 copy-start.4
  10.7 0.9 copy-start.6
  11.5 0.8 copy-start.7
  12.3 0.7 copy-start.9
  13.0 0.7 copy-start.10
  13.7 0.7 copy-start.11
  14.4 0.7 copy-start.13
  15.1 0.7 copy-start.14
  42.5 6.2 %copy-start.15 = (f32[32,8,64,256]{3,2,1,0:T(8,128)}, f32[32,8,64,256]{3,2,1,0:T(8,128)S(1)}, u32[]{:S(2)}) copy-start(f32[32,8,64,256]{3,2,1,0:T(8,128)S(1)} %multiply_add_fusion) | copy-start | bytes 50331652
  48.7 9.9 %copy-start.16 = (f32[8]{0:T(128)S(1)}, f32[8]{0:T(128)}, u32[]{:S(2)}) copy-start(f32[8]{0:T(128)} %param.27) | copy-start | bytes 100
  48.7 10.1 %copy-start.5 = (bf16[32,512]{1,0:T(8,128)(2,1)S(1)}, bf16[32,512]{1,0:T(8,128)(2,1)}, u32[]{:S(2)}) copy-start(bf16[32,512]{1,0:T(8,128)(2,1)} %hid.3) | copy-start | bytes 98308
  48.7 10.1 %copy-start.8 = (f32[8192]{0:T(1024)S(1)}, f32[8192]{0:T(1024)}, u32[]{:S(2)}) copy-start(f32[8192]{0:T(1024)} %param.35) | copy-start | bytes 98308
  48.7 10.1 %copy-start.12 = (f32[512]{0:T(512)S(1)}, f32[512]{0:T(512)}, u32[]{:S(2)}) copy-start(f32[512]{0:T(512)} %param.33) | copy-start | bytes 6148

commit v2 on v1

--- a/solution.py
+++ b/solution.py
@@ -111,7 +111,7 @@
 F32 = jnp.float32
 BF16 = jnp.bfloat16
 VM = pl.BlockSpec(memory_space=pltpu.VMEM)
-HB = pl.BlockSpec(memory_space=pl.ANY)
+HB = pl.BlockSpec(memory_space=pltpu.HBM)
 
 
 def spot(z, x, c):
@@ -231,13 +231,62 @@
     return total / (1.0 + jnp.exp(-total))
 
 
+def per_channel(heads, shape):
+    count = heads.shape[1]
+    head = lax.broadcasted_iota(jnp.int32, shape, 1) // (shape[1] // count)
+    out = jnp.zeros(shape, F32)
+    for h in range(count):
+        out = jnp.where(head == h, heads[:, h : h + 1], out)
+    return out
+
+
+def state_kernel(
+    state, sizex, retain, skipx, gate, bc, cx, cb,
+    new_state, gated, cx_out, cb_out,
+):
+    @pl.when((pl.program_id(0) == 0) & (pl.program_id(1) == 0))
+    def _():
+        cx_out[...] = cx[...]
+        cb_out[...] = cb[...]
+
+    reqs, heads, chans, _ = state.shape
+    wide = heads * chans
+    copies = wide // reqs
+    sx = jnp.concatenate([sizex[...]] * copies, axis=0).T
+    rt = jnp.concatenate([retain[...]] * copies, axis=0).T
+    first = pl.multiple_of(pl.program_id(0) * reqs, reqs)
+    b_rows = jnp.concatenate([bc[0, pl.ds(first, reqs)], bc[1, pl.ds(first, reqs)]], axis=1)
+    c_rows = jnp.concatenate([bc[2, pl.ds(first, reqs)], bc[3, pl.ds(first, reqs)]], axis=1)
+    lane = lax.broadcasted_iota(jnp.int32, (chans, wide), 1)
+    cols = [jnp.zeros((chans, wide), F32) for _ in range(heads)]
+    for r in range(reqs):
+        for h in range(heads):
+            at = slice(h * chans, (h + 1) * chans)
+            fresh = rt[at, r : r + 1] * state[r, h] + sx[at, r : r + 1] * b_rows[r : r + 1]
+            new_state[r, h] = fresh
+            out = jnp.sum(fresh * c_rows[r : r + 1], axis=1, keepdims=True)
+            cols[h] = jnp.where(lane == r, out, cols[h])
+    out = jnp.concatenate(cols, axis=0).T[:reqs]
+    gated[...] = (out + skipx[...]) * gate[...]
+
+
 def front_kernel(
-    hid, gain, wz, wx, wbc, wdt, dtb, dec, cxw, cbw, cxs, cbs,
-    xconv, gate, step, retain, bc, cxn, cbn,
-    blocks, xn, wz_v, wx_v, wbc_v, bc_own, bc_got,
-    wsem, bsem, ag_s, ag_r, bc_s, bc_r,
+    hid, wz, wx, wbc, wdt, *rest,
 ):
+    smalls_in, rest = rest[:8], rest[8:]
+    skipx, gate, sizex, retain, bc, cxn, cbn = rest[:7]
+    blocks, xn, wz_v, wx_v, wbc_v, bc_own, bc_got = rest[7:14]
+    smalls, rest = rest[14:22], rest[22:]
+    wsem, bsem, hsem, ssem, ag_s, ag_r, bc_s, bc_r = rest
+    gain, dtb, dec, skip, cxw, cbw, cxs, cbs = smalls
     me, z, x, c = coords()
+    hid_cp = pltpu.make_async_copy(hid, blocks.at[me], hsem)
+    hid_cp.start()
+    small_cps = [
+        pltpu.make_async_copy(smalls_in[i], smalls[i], ssem.at[i]) for i in range(len(smalls))
+    ]
+    for cp in small_cps:
+        cp.start()
     rows = wx_v.shape[1]
     bc_cp = pltpu.make_async_copy(wbc, wbc_v, bsem)
     bc_cp.start()
@@ -249,9 +298,11 @@
             )
             cp.start()
             loads.append(cp)
-    blocks[me] = hid[...]
     greet(me)
+    hid_cp.wait()
     started = gather_blocks(blocks, ag_s, ag_r)
+    for cp in small_cps:
+        cp.wait()
     norm_blocks(blocks, gain, xn)
     width = hid.shape[1]
 
@@ -273,7 +324,7 @@
             bc_got[slot] = bc_own[...]
 
     def project(w_v, first):
-        acc = jnp.zeros(xconv.shape, F32)
+        acc = jnp.zeros(gate.shape, F32)
         for k in range(4):
             loads[first + k].wait()
             for j in range(4):
@@ -283,7 +334,7 @@
                 )
         return acc
 
-    acc = jnp.zeros(step.shape, F32)
+    acc = jnp.zeros((hid.shape[0], dtb.shape[1]), F32)
     for k in range(NDEV):
         acc += lax.dot_general(
             xn[k], wdt[:, k * width : (k + 1) * width], (((1,), (1,)), ((), ())),
@@ -291,9 +342,10 @@
         )
     raw = acc + dtb[...]
     size = jnp.maximum(raw, 0.0) + jnp.log1p(jnp.exp(-jnp.abs(raw)))
-    step[...] = size
-    retain[...] = jnp.exp(-size * dec[...])
-    xconv[...] = conv_rows(cxs, project(wx_v, 0).astype(BF16), cxw, cxn)
+    retain[...] = per_channel(jnp.exp(-size * dec[...]), gate.shape)
+    xv = conv_rows(cxs, project(wx_v, 0).astype(BF16), cxw, cxn)
+    sizex[...] = per_channel(size, gate.shape) * xv
+    skipx[...] = per_channel(jnp.broadcast_to(skip[...], size.shape), gate.shape) * xv
     zv = project(wz_v, 4)
     gate[...] = zv / (1.0 + jnp.exp(-zv))
 
@@ -304,7 +356,7 @@
         def _():
             remote(bc_own, bc_got.at[i], bc_s.at[0], bc_r.at[i], src).wait_recv()
 
-    bc[...] = bc_got[...]
+    bc[...] = bc_got[...].astype(F32)
     for i in range(4):
         dev = goal * 4 + i
 
@@ -317,12 +369,19 @@
 
 
 def back_kernel(
-    gated, ggain, hid, mgain, wo, wu, wd,
-    result,
+    gated, ggain_in, hid_in, mgain_in, wo, wu, wd,
+    result, ggain, hid, mgain,
     wo_v, wu_v, wd_v, y, act, parts, blocks, xn, sq_own, sq_got,
     csend, crecv, xsend, xrecv, zsend, zrecv,
-    wsem, sq_s, sq_r, ag_s, ag_r, rs1, rs2,
+    wsem, ssem, sq_s, sq_r, ag_s, ag_r, rs1, rs2,
 ):
+    small_cps = [
+        pltpu.make_async_copy(ggain_in, ggain, ssem.at[0]),
+        pltpu.make_async_copy(hid_in, hid, ssem.at[1]),
+        pltpu.make_async_copy(mgain_in, mgain, ssem.at[2]),
+    ]
+    for cp in small_cps:
+        cp.start()
     me, z, x, c = coords()
     cols = wo_v.shape[2]
     rows = wu_v.shape[1]
@@ -341,6 +400,8 @@
     for cp in loads.values():
         cp.start()
     g = gated[...]
+    for cp in small_cps:
+        cp.wait()
     y[...] = (g * ggain[...]).astype(BF16)
     sq_own[...] = jnp.broadcast_to(jnp.sum(g * g, axis=1, keepdims=True), sq_own.shape)
     greet(me)
@@ -407,18 +468,15 @@
     bcw = w_bc.shape[1]
     ff = w_up.shape[1]
     dma = pltpu.SemaphoreType.DMA
-    xconv, gate, step, retain, bc, cxn, cbn = pl.pallas_call(
+    skipx, gate, sizex, retain, bc, cxn, cbn = pl.pallas_call(
         front_kernel,
-        out_shape=[
-            jax.ShapeDtypeStruct((req, inner), F32),
-            jax.ShapeDtypeStruct((req, inner), F32),
-            jax.ShapeDtypeStruct((req, heads_dev), F32),
-            jax.ShapeDtypeStruct((req, heads_dev), F32),
-            jax.ShapeDtypeStruct((4, req, bcw), BF16),
+        out_shape=[jax.ShapeDtypeStruct((req, inner), F32)] * 4
+        + [
+            jax.ShapeDtypeStruct((4, req, bcw), F32),
             jax.ShapeDtypeStruct((3, req, inner), BF16),
             jax.ShapeDtypeStruct((3, req, bcw), BF16),
         ],
-        in_specs=[VM, VM, HB, HB, HB] + [VM] * 7,
+        in_specs=[HB] * 4 + [VM] + [HB] * 8,
         out_specs=[VM] * 7,
         scratch_shapes=[
             pltpu.VMEM((NDEV, req, width), BF16),
@@ -428,36 +486,58 @@
             pltpu.VMEM((dim, bcw), BF16),
             pltpu.VMEM((req, bcw), BF16),
             pltpu.VMEM((4, req, bcw), BF16),
-            dma((8,)), dma, dma((15,)), dma((16,)), dma((4,)), dma((4,)),
+            pltpu.VMEM((1, dim), F32),
+            pltpu.VMEM((1, heads_dev), F32),
+            pltpu.VMEM((1, heads_dev), F32),
+            pltpu.VMEM((1, heads_dev), F32),
+            pltpu.VMEM((4, inner), F32),
+            pltpu.VMEM((4, bcw), F32),
+            pltpu.VMEM((3, req, inner), BF16),
+            pltpu.VMEM((3, req, bcw), BF16),
+            dma((8,)), dma, dma, dma((8,)), dma((15,)), dma((16,)), dma((4,)), dma((4,)),
         ],
         compiler_params=pltpu.CompilerParams(
-            collective_id=0, has_side_effects=True, vmem_limit_bytes=32 << 20
+            collective_id=0, has_side_effects=True, vmem_limit_bytes=63 << 20
         ),
         name="front",
     )(
-        hidden, norm_in_gain[None], w_z, w_x, w_bc, w_dt.T, dt_bias[None], decay_rate[None],
-        conv_x_weight, conv_bc_weight,
+        hidden, w_z, w_x, w_bc, w_dt.T, norm_in_gain[None], dt_bias[None], decay_rate[None],
+        skip_gain[None], conv_x_weight, conv_bc_weight,
         conv_x_state.transpose(1, 0, 2), conv_bc_state.transpose(1, 0, 2),
     )
-    b_part = jnp.concatenate([bc[0], bc[1]], axis=1).astype(F32)
-    c_part = jnp.concatenate([bc[2], bc[3]], axis=1).astype(F32)
-    x_heads = xconv.reshape(req, heads_dev, HEAD_DIM)
-    ssm_new = (
-        retain[:, :, None, None] * ssm_state
-        + (step[:, :, None] * x_heads)[..., None] * b_part[:, None, None, :]
-    )
-    head_out = (
-        jnp.einsum("rhpn,rn->rhp", ssm_new, c_part, precision=lax.Precision.HIGHEST)
-        + skip_gain[None, :, None] * x_heads
-    )
-    gated = head_out.reshape(req, inner) * gate
+    some = 8
+    pair = 128 // HEAD_DIM
+    chan = pl.BlockSpec((some, 128), lambda i, j: (i, j))
+    held = pl.BlockSpec((some, pair, HEAD_DIM, N), lambda i, j: (i, j, 0, 0))
+    whole = [
+        pl.BlockSpec((4, req, bcw), lambda i, j: (0, 0, 0)),
+        pl.BlockSpec((3, req, inner), lambda i, j: (0, 0, 0)),
+        pl.BlockSpec((3, req, bcw), lambda i, j: (0, 0, 0)),
+    ]
+    ssm_new, gated, cxn, cbn = pl.pallas_call(
+        state_kernel,
+        grid=(req // some, heads_dev // pair),
+        out_shape=[
+            jax.ShapeDtypeStruct(ssm_state.shape, F32),
+            jax.ShapeDtypeStruct((req, inner), F32),
+            jax.ShapeDtypeStruct((3, req, inner), BF16),
+            jax.ShapeDtypeStruct((3, req, bcw), BF16),
+        ],
+        in_specs=[held] + [chan] * 4 + whole,
+        out_specs=[held, chan] + whole[1:],
+        compiler_params=pltpu.CompilerParams(vmem_limit_bytes=63 << 20),
+        name="state",
+    )(ssm_state, sizex, retain, skipx, gate, bc, cxn, cbn)
     slot = (LINES, req, width)
     result = pl.pallas_call(
         back_kernel,
         out_shape=jax.ShapeDtypeStruct((req, width), BF16),
-        in_specs=[VM] * 4 + [HB] * 3,
+        in_specs=[VM] + [HB] * 6,
         out_specs=VM,
         scratch_shapes=[
+            pltpu.VMEM((1, inner), F32),
+            pltpu.VMEM((req, width), BF16),
+            pltpu.VMEM((1, dim), F32),
             pltpu.VMEM((4, inner, dim // 4), BF16),
             pltpu.VMEM((4, dim // 4, ff), BF16),
             pltpu.VMEM((4, ff, dim // 4), BF16),
@@ -474,10 +554,10 @@
             pltpu.VMEM((2,) + slot, BF16),
             pltpu.VMEM((2,) + slot, BF16),
             pltpu.VMEM((2,) + slot, BF16),
-            dma((12,)), dma((3,)), dma((3,)), dma((15,)), dma((16,)), dma((6, 4)), dma((6, 4)),
+            dma((12,)), dma((3,)), dma((3,)), dma((3,)), dma((15,)), dma((16,)), dma((6, 4)), dma((6, 4)),
         ],
         compiler_params=pltpu.CompilerParams(
-            collective_id=1, has_side_effects=True, vmem_limit_bytes=52 << 20
+            collective_id=1, has_side_effects=True, vmem_limit_bytes=63 << 20
         ),
         name="back",
     )(gated, group_gain[None], hidden, norm_mid_gain[None], w_out, w_up, w_down)

time: 101 us -> 110 us (1.089)
  Pallas kernels: 58.5 us -> 107 us
  local copies, waits for them, and re-layouts: 23.3 us -> 1.38 us
  matrix products: 9.84 us -> 0 us
  other arithmetic: 7.86 us -> 0 us
    pallas_call x0 -> x1, Pallas kernels: none -> 32.8 us  [body(): pl.pallas_call(state_kernel, grid=(req // some, heads_dev // pair), out_s...]
    unnamed x37 -> x1, local copies, waits for them, and re-layouts: 23.1 us -> 1.38 us
    pallas_call x1, Pallas kernels: 39.7 us -> 51.7 us  [body(): pl.pallas_call(back_kernel, out_shape=jax.ShapeDtypeStruct((req, width),...]
    dot_general x1 -> x0, matrix products: 9.84 us -> none  [body(): jnp.einsum('rhpn,rn->rhp', ssm_new, c_part, precision=lax.Precision.HIGHEST)]
    add x2 -> x0, other arithmetic: 7.74 us -> none  [the longest x1 7.65 us: body(): retain[:, :, None, None] * ssm_state]
    pallas_call x1, Pallas kernels: 18.9 us -> 23 us  [body(): pl.pallas_call(front_kernel, out_shape=[jax.ShapeDtypeStruct((req, inner)...]
where the time goes in v2:
time: 110 us; the launch traced here: 109 us
  Pallas kernels  107 us (97%)
  local copies, waits for them, and re-layouts  1.38 us (1%)
    pallas_call x1, Pallas kernels, body(): pl.pallas_call(back_kernel, out_shape=jax.ShapeDtypeStruct((req, width),...  51.7 us
    pallas_call x1, Pallas kernels, body(): pl.pallas_call(state_kernel, grid=(req // some, heads_dev // pair), out_s...  32.8 us
    pallas_call x1, Pallas kernels, body(): pl.pallas_call(front_kernel, out_shape=[jax.ShapeDtypeStruct((req, inner)...  23 us

profile of v2, /device:TPU:0, one launch (start us, length us, event | category | flops | bytes accessed | tf_op | source)
XLA Modules:
  0.0 109.5 jit_solution(9212580156752389699)
XLA Ops:
  0.6 23.0 %front.1 = (f32[32,512]{1,0:T(8,128)}, f32[32,512]{1,0:T(8,128)}, f32[32,512]{1,0:T(8,128)}, f32[32,512]{1,0:T(8,128)}, f32[4,32,128]{2,1,0:T(8,128)}, /*index=5...) custom-call(bf16[32,512]{1,0:T(8,128)(2,1)} %hid_in.1, bf16[8192,512]{1,0:T(8,128)(2,1)} %wz.1, bf16[8192,512]{1,0:T(8,128)(2,1)} %wx.1, ...), custom_call_target="tpu_custom_call" | custom-call | tf_op jit(solution)/shard_map/front/pallas_call | solution.py:471
  23.6 32.8 %state.2 = (f32[32,8,64,256]{3,2,1,0:T(8,128)}, f32[32,512]{1,0:T(8,128)}, bf16[3,32,512]{2,1,0:T(8,128)(2,1)}, bf16[3,32,128]{2,1,0:T(8,128)(2,1)}) custom-call(f32[32,8,64,256]{3,2,1,0:T(8,128)} %state.3, f32[32,512]{1,0:T(8,128)} %get-tuple-element.15.sizex, f32[32,512]{1,0:T(8,128)} %get-tuple-element.16.retain, f32[32,512]{1,0:T(8,128)} %get-tuple-element.17.skipx, ...), custom_call_target="tpu_custom_call" | custom-call | tf_op jit(solution)/shard_map/state/pallas_call | solution.py:517
  56.4 51.7 %back.1 = bf16[32,512]{1,0:T(8,128)(2,1)} custom-call(f32[32,512]{1,0:T(8,128)} %get-tuple-element.22.gated, f32[1,512]{1,0:T(1,128)} %bitcast.16, bf16[32,512]{1,0:T(8,128)(2,1)} %hid_in.1, f32[1,8192]{1,0:T(1,128)} %bitcast.14, bf16[512,8192]{1,0:T(8,128)(2,1)} %wo.1, bf16[8192,1024]{1,0:T(8,128)(2,1)} %wu.1, bf16[1024,8192]{1,0:T(8,128)(2,1)} %wd.1), custom_call_target="tpu_custom_call" | custom-call | tf_op jit(solution)/shard_map/back/pallas_call | solution.py:532
  108.1 1.4 %copy.24 = bf16[32,512]{1,0:T(8,128)(2,1)} copy(bf16[32,512]{1,0:T(8,128)(2,1)} %back.1) | data formatting | bytes 65536

commit v3 on v1

--- a/solution.py
+++ b/solution.py
@@ -111,7 +111,7 @@
 F32 = jnp.float32
 BF16 = jnp.bfloat16
 VM = pl.BlockSpec(memory_space=pltpu.VMEM)
-HB = pl.BlockSpec(memory_space=pl.ANY)
+HB = pl.BlockSpec(memory_space=pltpu.HBM)
 
 
 def spot(z, x, c):
@@ -232,12 +232,22 @@
 
 
 def front_kernel(
-    hid, gain, wz, wx, wbc, wdt, dtb, dec, cxw, cbw, cxs, cbs,
-    xconv, gate, step, retain, bc, cxn, cbn,
-    blocks, xn, wz_v, wx_v, wbc_v, bc_own, bc_got,
-    wsem, bsem, ag_s, ag_r, bc_s, bc_r,
+    hid, wz, wx, wbc, wdt, *rest,
 ):
+    smalls_in, rest = rest[:7], rest[7:]
+    xconv, gate, step, retain, bc, cxn, cbn = rest[:7]
+    blocks, xn, wz_v, wx_v, wbc_v, bc_own, bc_got = rest[7:14]
+    smalls, rest = rest[14:21], rest[21:]
+    wsem, bsem, hsem, ssem, ag_s, ag_r, bc_s, bc_r = rest
+    gain, dtb, dec, cxw, cbw, cxs, cbs = smalls
     me, z, x, c = coords()
+    hid_cp = pltpu.make_async_copy(hid, blocks.at[me], hsem)
+    hid_cp.start()
+    small_cps = [
+        pltpu.make_async_copy(smalls_in[i], smalls[i], ssem.at[i]) for i in range(len(smalls))
+    ]
+    for cp in small_cps:
+        cp.start()
     rows = wx_v.shape[1]
     bc_cp = pltpu.make_async_copy(wbc, wbc_v, bsem)
     bc_cp.start()
@@ -249,9 +259,11 @@
             )
             cp.start()
             loads.append(cp)
-    blocks[me] = hid[...]
     greet(me)
+    hid_cp.wait()
     started = gather_blocks(blocks, ag_s, ag_r)
+    for cp in small_cps:
+        cp.wait()
     norm_blocks(blocks, gain, xn)
     width = hid.shape[1]
 
@@ -273,7 +285,7 @@
             bc_got[slot] = bc_own[...]
 
     def project(w_v, first):
-        acc = jnp.zeros(xconv.shape, F32)
+        acc = jnp.zeros(gate.shape, F32)
         for k in range(4):
             loads[first + k].wait()
             for j in range(4):
@@ -283,7 +295,7 @@
                 )
         return acc
 
-    acc = jnp.zeros(step.shape, F32)
+    acc = jnp.zeros((hid.shape[0], dtb.shape[1]), F32)
     for k in range(NDEV):
         acc += lax.dot_general(
             xn[k], wdt[:, k * width : (k + 1) * width], (((1,), (1,)), ((), ())),
@@ -317,12 +329,19 @@
 
 
 def back_kernel(
-    gated, ggain, hid, mgain, wo, wu, wd,
-    result,
+    gated, ggain_in, hid_in, mgain_in, wo, wu, wd,
+    result, ggain, hid, mgain,
     wo_v, wu_v, wd_v, y, act, parts, blocks, xn, sq_own, sq_got,
     csend, crecv, xsend, xrecv, zsend, zrecv,
-    wsem, sq_s, sq_r, ag_s, ag_r, rs1, rs2,
+    wsem, ssem, sq_s, sq_r, ag_s, ag_r, rs1, rs2,
 ):
+    small_cps = [
+        pltpu.make_async_copy(ggain_in, ggain, ssem.at[0]),
+        pltpu.make_async_copy(hid_in, hid, ssem.at[1]),
+        pltpu.make_async_copy(mgain_in, mgain, ssem.at[2]),
+    ]
+    for cp in small_cps:
+        cp.start()
     me, z, x, c = coords()
     cols = wo_v.shape[2]
     rows = wu_v.shape[1]
@@ -341,6 +360,8 @@
     for cp in loads.values():
         cp.start()
     g = gated[...]
+    for cp in small_cps:
+        cp.wait()
     y[...] = (g * ggain[...]).astype(BF16)
     sq_own[...] = jnp.broadcast_to(jnp.sum(g * g, axis=1, keepdims=True), sq_own.shape)
     greet(me)
@@ -409,16 +430,14 @@
     dma = pltpu.SemaphoreType.DMA
     xconv, gate, step, retain, bc, cxn, cbn = pl.pallas_call(
         front_kernel,
-        out_shape=[
-            jax.ShapeDtypeStruct((req, inner), F32),
-            jax.ShapeDtypeStruct((req, inner), F32),
-            jax.ShapeDtypeStruct((req, heads_dev), F32),
-            jax.ShapeDtypeStruct((req, heads_dev), F32),
+        out_shape=[jax.ShapeDtypeStruct((req, inner), F32)] * 2
+        + [jax.ShapeDtypeStruct((req, heads_dev), F32)] * 2
+        + [
             jax.ShapeDtypeStruct((4, req, bcw), BF16),
             jax.ShapeDtypeStruct((3, req, inner), BF16),
             jax.ShapeDtypeStruct((3, req, bcw), BF16),
         ],
-        in_specs=[VM, VM, HB, HB, HB] + [VM] * 7,
+        in_specs=[HB] * 4 + [VM] + [HB] * 7,
         out_specs=[VM] * 7,
         scratch_shapes=[
             pltpu.VMEM((NDEV, req, width), BF16),
@@ -428,14 +447,21 @@
             pltpu.VMEM((dim, bcw), BF16),
             pltpu.VMEM((req, bcw), BF16),
             pltpu.VMEM((4, req, bcw), BF16),
-            dma((8,)), dma, dma((15,)), dma((16,)), dma((4,)), dma((4,)),
+            pltpu.VMEM((1, dim), F32),
+            pltpu.VMEM((1, heads_dev), F32),
+            pltpu.VMEM((1, heads_dev), F32),
+            pltpu.VMEM((4, inner), F32),
+            pltpu.VMEM((4, bcw), F32),
+            pltpu.VMEM((3, req, inner), BF16),
+            pltpu.VMEM((3, req, bcw), BF16),
+            dma((8,)), dma, dma, dma((7,)), dma((15,)), dma((16,)), dma((4,)), dma((4,)),
         ],
         compiler_params=pltpu.CompilerParams(
-            collective_id=0, has_side_effects=True, vmem_limit_bytes=32 << 20
+            collective_id=0, has_side_effects=True, vmem_limit_bytes=63 << 20
         ),
         name="front",
     )(
-        hidden, norm_in_gain[None], w_z, w_x, w_bc, w_dt.T, dt_bias[None], decay_rate[None],
+        hidden, w_z, w_x, w_bc, w_dt.T, norm_in_gain[None], dt_bias[None], decay_rate[None],
         conv_x_weight, conv_bc_weight,
         conv_x_state.transpose(1, 0, 2), conv_bc_state.transpose(1, 0, 2),
     )
@@ -455,9 +481,12 @@
     result = pl.pallas_call(
         back_kernel,
         out_shape=jax.ShapeDtypeStruct((req, width), BF16),
-        in_specs=[VM] * 4 + [HB] * 3,
+        in_specs=[VM] + [HB] * 3 + [pl.BlockSpec(memory_space=pl.ANY)] * 3,
         out_specs=VM,
         scratch_shapes=[
+            pltpu.VMEM((1, inner), F32),
+            pltpu.VMEM((req, width), BF16),
+            pltpu.VMEM((1, dim), F32),
             pltpu.VMEM((4, inner, dim // 4), BF16),
             pltpu.VMEM((4, dim // 4, ff), BF16),
             pltpu.VMEM((4, ff, dim // 4), BF16),
@@ -474,7 +503,7 @@
             pltpu.VMEM((2,) + slot, BF16),
             pltpu.VMEM((2,) + slot, BF16),
             pltpu.VMEM((2,) + slot, BF16),
-            dma((12,)), dma((3,)), dma((3,)), dma((15,)), dma((16,)), dma((6, 4)), dma((6, 4)),
+            dma((12,)), dma((3,)), dma((3,)), dma((3,)), dma((15,)), dma((16,)), dma((6, 4)), dma((6, 4)),
         ],
         compiler_params=pltpu.CompilerParams(
             collective_id=1, has_side_effects=True, vmem_limit_bytes=52 << 20

time: 101 us -> 90.2 us (0.89)
  local copies, waits for them, and re-layouts: 23.3 us -> 9.82 us
  Pallas kernels: 58.5 us -> 61 us
    unnamed x37 -> x19, local copies, waits for them, and re-layouts: 23.1 us -> 8.05 us
    pallas_call x1, Pallas kernels: 18.9 us -> 22.8 us  [body(): pl.pallas_call(front_kernel, out_shape=[jax.ShapeDtypeStruct((req, inner)...]
    pallas_call x1, Pallas kernels: 39.7 us -> 38.2 us  [body(): pl.pallas_call(back_kernel, out_shape=jax.ShapeDtypeStruct((req, width),...]
where the time goes in v3:
time: 90.2 us; the launch traced here: 89.9 us
  Pallas kernels  61 us (68%)
  matrix products  9.84 us (11%)
  local copies, waits for them, and re-layouts  9.82 us (11%)
  other arithmetic  8.44 us (9%)
    pallas_call x1, Pallas kernels, body(): pl.pallas_call(back_kernel, out_shape=jax.ShapeDtypeStruct((req, width),...  38.2 us
    pallas_call x1, Pallas kernels, body(): pl.pallas_call(front_kernel, out_shape=[jax.ShapeDtypeStruct((req, inner)...  22.8 us
    dot_general x1, matrix products, body(): jnp.einsum('rhpn,rn->rhp', ssm_new, c_part, precision=lax.Precision.HIGHEST)  9.84 us
    unnamed x19, local copies, waits for them, and re-layouts  8.05 us
    add x1, other arithmetic, body(): retain[:, :, None, None] * ssm_state  7.52 us

profile of v3, /device:TPU:0, one launch (start us, length us, event | category | flops | bytes accessed | tf_op | source)
XLA Modules:
  0.0 89.9 jit_solution(11559334882387396962)
XLA Ops:
  0.6 22.8 %front.1 = (f32[32,512]{1,0:T(8,128)}, f32[32,512]{1,0:T(8,128)}, f32[32,8]{1,0:T(8,128)}, f32[32,8]{1,0:T(8,128)}, bf16[4,32,128]{2,1,0:T(8,128)(2,1)}, /*index...) custom-call(bf16[32,512]{1,0:T(8,128)(2,1)} %hid_in.1, bf16[8192,512]{1,0:T(8,128)(2,1)} %wz.1, bf16[8192,512]{1,0:T(8,128)(2,1)} %wx.1, ...), custom_call_target="tpu_custom_call" | custom-call | tf_op jit(solution)/shard_map/front/pallas_call | solution.py:431
  23.4 0.8 slice_bitcast_fusion.1
  24.2 0.9 %reshape.39 = f32[32,8,64]{2,1,0:T(8,128)S(1)} reshape(f32[32,512]{1,0:T(8,128)} %get-tuple-element.13) | data formatting | bytes 131072 | tf_op jit(solution)/shard_map/reshape | solution.py:470
  25.1 0.8 broadcast_multiply_fusion
  25.9 7.5 %multiply_add_fusion = f32[32,8,64,256]{3,2,1,0:T(8,128)S(1)} fusion(f32[32,8,64,256]{3,2,1,0:T(8,128)} %param.32, f32[32,256]{1,0:T(8,128)S(1)} %maximum_convert_fusion, f32[32,8,64]{2,1,0:T(8,128)S(1)} %broadcast_multiply_fusion, f32[32,8]{1,0:T(8,128)} %get-tuple-element.11), kind=kLoop, calls=%fused_computation | loop fusion | flops 12582912 | bytes 33653760 | tf_op jit(solution)/shard_map/add | solution.py:472
  33.5 0.0 copy-start.3
  33.5 6.2 %copy-done.3 = f32[32,8,64,256]{3,2,1,0:T(8,128)} copy-done((f32[32,8,64,256]{3,2,1,0:T(8,128)}, f32[32,8,64,256]{3,2,1,0:T(8,128)S(1)}, u32[]{:S(2)}) %copy-start.3) | copy-done | bytes 16777240
  39.6 0.0 copy-start.2
  39.6 9.8 %fusion = f32[32,1,8,64]{3,1,2,0:T(1,128)S(1)} fusion(f32[32,8,64,256]{3,2,1,0:T(8,128)S(1)} %multiply_add_fusion, bf16[32,256,1,1]{1,0,2,3:T(8,128)(2,1)S(1)} %maximum_bitcast_fusion), kind=kOutput, calls=%fused_computation.3 | convolution fusion | flops 50331648 | bytes 16859136 | tf_op jit(solution)/shard_map/rhpn,rn->rhp/dot_general | solution.py:476
  49.5 0.0 copy-done.7
  49.5 0.1 multiply_add_fusion.1
  49.6 0.1 reshape.40
  49.7 0.0 copy-done.5
  49.7 0.0 copy-done
  49.7 0.0 copy-done.1
  49.7 0.0 copy-done.2
  49.7 0.0 copy-start.4
  49.7 0.0 copy-start.6
  49.8 38.2 %back.1 = bf16[32,512]{1,0:T(8,128)(2,1)S(1)} custom-call(f32[32,512]{1,0:T(8,128)S(1)} %mul.53.gated, f32[1,512]{1,0:T(1,128)S(1)} %bitcast.24, bf16[32,512]{1,0:T(8,128)(2,1)S(1)} %copy-done, f32[1,8192]{1,0:T(1,128)S(1)} %bitcast.23, bf16[512,8192]{1,0:T(8,128)(2,1)} %wo.1, bf16[8192,1024]{1,0:T(8,128)(2,1)} %wu.1, bf16[1024,8192]{1,0:T(8,128)(2,1)} %wd.1), custom_call_target="tpu_custom_call" | custom-call | tf_op jit(solution)/shard_map/back/pallas_call | solution.py:481
  88.0 0.6 copy.30
  88.6 0.0 copy-done.4
  88.6 0.6 copy.31
  89.3 0.0 copy-done.6
  89.3 0.6 copy.32
  (7 shorter events, 0.0 us)
Async XLA Ops:
  33.5 6.2 %copy-start.3 = (f32[32,8,64,256]{3,2,1,0:T(8,128)}, f32[32,8,64,256]{3,2,1,0:T(8,128)S(1)}, u32[]{:S(2)}) copy-start(f32[32,8,64,256]{3,2,1,0:T(8,128)S(1)} %multiply_add_fusion) | copy-start | bytes 50331652
  39.6 9.9 %copy-start.7 = (f32[8]{0:T(128)S(1)}, f32[8]{0:T(128)}, u32[]{:S(2)}) copy-start(f32[8]{0:T(128)} %param.27) | copy-start | bytes 100
  39.6 10.1 %copy-start.5 = (f32[32,512]{1,0:T(8,128)S(1)}, f32[32,512]{1,0:T(8,128)}, u32[]{:S(2)}) copy-start(f32[32,512]{1,0:T(8,128)} %get-tuple-element.15) | copy-start | bytes 196612
  39.6 10.1 %copy-start = (bf16[32,512]{1,0:T(8,128)(2,1)S(1)}, bf16[32,512]{1,0:T(8,128)(2,1)}, u32[]{:S(2)}) copy-start(bf16[32,512]{1,0:T(8,128)(2,1)} %hid_in.1) | copy-start | bytes 98308
  39.6 10.1 %copy-start.1 = (f32[8192]{0:T(1024)S(1)}, f32[8192]{0:T(1024)}, u32[]{:S(2)}) copy-start(f32[8192]{0:T(1024)} %param.35) | copy-start | bytes 98308
  39.6 10.1 %copy-start.2 = (f32[512]{0:T(512)S(1)}, f32[512]{0:T(512)}, u32[]{:S(2)}) copy-start(f32[512]{0:T(512)} %param.33) | copy-start | bytes 6148
  49.7 38.9 %copy-start.4 = (bf16[3,32,512]{2,1,0:T(8,128)(2,1)S(1)}, bf16[3,32,512]{2,1,0:T(8,128)(2,1)}, u32[]{:S(2)}) copy-start(bf16[3,32,512]{2,1,0:T(8,128)(2,1)} %get-tuple-element.16) | copy-start | bytes 294916
  49.7 39.5 %copy-start.6 = (bf16[3,32,128]{2,1,0:T(8,128)(2,1)S(1)}, bf16[3,32,128]{2,1,0:T(8,128)(2,1)}, u32[]{:S(2)}) copy-start(bf16[3,32,128]{2,1,0:T(8,128)(2,1)} %get-tuple-element.17) | copy-start | bytes 73732
